TPU v7x, 32 devices: a whole 2x2x4 slice. The times are simulated.
32 devices in a mesh: groups: 2 (over x), dap: 16 (over z, y, core).
Axes of the slice: x: 2, y: 2, z: 4, core: 2. Of those that a mesh axis runs over, the one named last changes fastest.
Arguments:
- pair_state: bfloat16 [160, 80, 128], P(('groups', 'dap')), parts along dimension 0, may hold values from -6 to 6
- chain_index: int32 [160], P('groups'), parts along dimension 0, may hold values from 0 to 3, as said below
- pair_mask: int32 [160, 80], P(('groups', 'dap')), parts along dimension 0, may hold values 0 or 1
- chain_table: float32 [2, 128], replicated, may hold values from -4 to 4
- norm_gain: float32 [2, 2, 128], replicated, may hold values from 0.1 to 1.9
- norm_shift: float32 [2, 2, 128], replicated, may hold values from -3 to 3
- projections: bfloat16 [2, 5, 128, 128], replicated, may hold values from -0.5 to 0.5
- output_weight: bfloat16 [2, 128, 128], replicated, may hold values from -0.5 to 0.5
- cotangent: bfloat16 [160, 80, 128], P(('groups', 'dap')), parts along dimension 0, may hold values from -6 to 6
Outputs:
- grad_pair: bfloat16 [160, 80, 128], P(('groups', 'dap')), parts along dimension 0
- projection_grads: float32 [4, 5, 128, 128], P('groups'), parts along dimension 0
- output_weight_grad: float32 [4, 128, 128], P('groups'), parts along dimension 0
There are 2 independent parts, one for each index of `groups`. A program takes and returns all parts, laid end to end along the dimension named above; an argument that names none is the same for every part. Nothing has to cross between parts.
Inputs may be any that keep to these rules, and one draw needn't show every extreme that they name: `chain_index`: the chain index never decreases along the residues, and every chain has at least one residue.
All inputs are finite; a program needn't handle non-finite values. No bound on the sum of `pair_mask` on one device may be relied on, other than what follows from the above.
Results may differ from a plain program's by a relative error of at most 0.007.
Values may be sent and summed in bfloat16 or wider, within the bound.
A program may use at most 128 MiB of HBM per device.

v0:
```python
import jax
import jax.numpy as jnp
from jax import lax
from jax.sharding import PartitionSpec as P

EPSILON = 1e-05


def normalize(values, norm_gain, norm_shift, reduce_axis):
    center = values - jnp.mean(values, axis=reduce_axis, keepdims=True)
    inverse = lax.rsqrt(jnp.mean(center * center, axis=reduce_axis, keepdims=True) + EPSILON)
    normed = center * inverse
    return (normed, inverse, normed * norm_gain + norm_shift)


def normalize_back(grad_output, normed, inverse, norm_gain, reduce_axis):
    scaled = grad_output * norm_gain
    centered = scaled - jnp.mean(scaled, axis=reduce_axis, keepdims=True)
    return (
        centered - normed * jnp.mean(scaled * normed, axis=reduce_axis, keepdims=True)
    ) * inverse


def multiply(left_cols, right_cols, incoming):
    if incoming:
        return jnp.einsum(
            "xcki,xckj->xcij", left_cols, right_cols, preferred_element_type=jnp.float32
        )
    return jnp.einsum("xcik,xcjk->xcij", left_cols, right_cols, preferred_element_type=jnp.float32)


def factor_grads(grad_cols, left_cols, right_cols, incoming):
    if incoming:
        left_grad = jnp.einsum(
            "xcij,xckj->xcki", grad_cols, right_cols, preferred_element_type=jnp.float32
        )
        right_grad = jnp.einsum(
            "xcij,xcki->xckj", grad_cols, left_cols, preferred_element_type=jnp.float32
        )
    else:
        left_grad = jnp.einsum(
            "xcij,xcjk->xcik", grad_cols, right_cols, preferred_element_type=jnp.float32
        )
        right_grad = jnp.einsum(
            "xcij,xcik->xcjk", grad_cols, left_cols, preferred_element_type=jnp.float32
        )
    return (left_grad.astype(jnp.bfloat16), right_grad.astype(jnp.bfloat16))


def block_forward(stream, masked, norm_gains, norm_shifts, weights, out_weight, incoming):
    rows, residues, channels = stream.shape
    devices = lax.axis_size("dap")
    slices = channels // devices
    normed_in, inverse_in, scaled_in = normalize(stream, norm_gains[0], norm_shifts[0], 2)
    activated = scaled_in.astype(jnp.bfloat16)
    factor_pre = jnp.einsum(
        "rnd,pdc->pcrn", activated, weights[:4], preferred_element_type=jnp.float32
    )
    gate_pre = jnp.einsum("rnd,dc->rnc", activated, weights[4], preferred_element_type=jnp.float32)
    gate_left = jax.nn.sigmoid(factor_pre[1])
    gate_right = jax.nn.sigmoid(factor_pre[3])
    left_factor = (masked * gate_left * factor_pre[0]).astype(jnp.bfloat16)
    right_factor = (masked * gate_right * factor_pre[2]).astype(jnp.bfloat16)
    left_blocks = left_factor.reshape(devices, slices, rows, residues)
    right_blocks = right_factor.reshape(devices, slices, rows, residues)
    left_cols, right_cols = (
        lax.all_to_all(left_blocks, "dap", split_axis=0, concat_axis=2, tiled=True),
        lax.all_to_all(right_blocks, "dap", split_axis=0, concat_axis=2, tiled=True),
    )
    product = multiply(left_cols, right_cols, incoming).astype(jnp.bfloat16)
    returned = lax.all_to_all(product, "dap", split_axis=2, concat_axis=0, tiled=True)
    product_rows = returned.reshape(channels, rows, residues)
    normed_out, inverse_out, scaled_out = normalize(
        product_rows.astype(jnp.float32),
        norm_gains[1][:, None, None],
        norm_shifts[1][:, None, None],
        0,
    )
    mixture = scaled_out.astype(jnp.bfloat16)
    update = jnp.einsum("crn,cd->rnd", mixture, out_weight, preferred_element_type=jnp.float32)
    out_gate = jax.nn.sigmoid(gate_pre)
    following = (stream + out_gate * update).astype(jnp.bfloat16)
    stored = (
        activated,
        factor_pre,
        left_cols,
        right_cols,
        normed_out,
        inverse_out,
        mixture,
        update,
        out_gate,
        normed_in,
        inverse_in,
    )
    return (following, stored)


def block_backward(upstream, stored, masked, norm_gains, weights, out_weight, incoming):
    (
        activated,
        factor_pre,
        left_cols,
        right_cols,
        normed_out,
        inverse_out,
        mixture,
        update,
        out_gate,
        normed_in,
        inverse_in,
    ) = stored
    rows, residues, channels = upstream.shape
    devices = lax.axis_size("dap")
    slices = channels // devices
    update_grad = (upstream * out_gate).astype(jnp.bfloat16)
    gate_grad = (upstream * update * out_gate * (1.0 - out_gate)).astype(jnp.bfloat16)
    out_weight_grad = jnp.einsum(
        "crn,rnd->cd", mixture, update_grad, preferred_element_type=jnp.float32
    )
    mixture_grad = jnp.einsum(
        "rnd,cd->crn", update_grad, out_weight, preferred_element_type=jnp.float32
    )
    product_grad = normalize_back(
        mixture_grad, normed_out, inverse_out, norm_gains[1][:, None, None], 0
    ).astype(jnp.bfloat16)
    grad_blocks = product_grad.reshape(devices, slices, rows, residues)
    grad_cols = lax.all_to_all(grad_blocks, "dap", split_axis=0, concat_axis=2, tiled=True)
    left_grad, right_grad = factor_grads(grad_cols, left_cols, right_cols, incoming)
    left_back, right_back = (
        lax.all_to_all(left_grad, "dap", split_axis=2, concat_axis=0, tiled=True),
        lax.all_to_all(right_grad, "dap", split_axis=2, concat_axis=0, tiled=True),
    )
    left_rows = left_back.reshape(channels, rows, residues).astype(jnp.float32)
    right_rows = right_back.reshape(channels, rows, residues).astype(jnp.float32)
    gate_left = jax.nn.sigmoid(factor_pre[1])
    gate_right = jax.nn.sigmoid(factor_pre[3])
    factor_grad = jnp.stack(
        [
            left_rows * masked * gate_left,
            left_rows * masked * factor_pre[0] * gate_left * (1.0 - gate_left),
            right_rows * masked * gate_right,
            right_rows * masked * factor_pre[2] * gate_right * (1.0 - gate_right),
        ]
    ).astype(jnp.bfloat16)
    factor_weight_grads = jnp.einsum(
        "rnd,pcrn->pdc", activated, factor_grad, preferred_element_type=jnp.float32
    )
    gate_weight_grad = jnp.einsum(
        "rnd,rnc->dc", activated, gate_grad, preferred_element_type=jnp.float32
    )
    weight_grads = jnp.concatenate([factor_weight_grads, gate_weight_grad[None]], 0)
    input_grad = jnp.einsum(
        "pcrn,pdc->rnd", factor_grad, weights[:4], preferred_element_type=jnp.float32
    )
    input_grad = input_grad + jnp.einsum(
        "rnc,dc->rnd", gate_grad, weights[4], preferred_element_type=jnp.float32
    )
    stream_grad = upstream + normalize_back(input_grad, normed_in, inverse_in, norm_gains[0], 2)
    return (stream_grad, weight_grads, out_weight_grad)


def reduce_block(weight_grads, out_weight_grad):
    return lax.psum((weight_grads, out_weight_grad), "dap")


def shards(
    pair_state,
    chain_index,
    pair_mask,
    chain_table,
    norm_gain,
    norm_shift,
    projections,
    output_weight,
    cotangent,
):
    rows, residues, channels = pair_state.shape
    first_row = lax.axis_index("dap") * rows
    own_chain = lax.dynamic_slice_in_dim(chain_index, first_row, rows, 0)
    same_chain = own_chain[:, None] == chain_index[None, :]
    stream = pair_state.astype(jnp.float32) + jnp.where(
        same_chain[:, :, None], chain_table[1], chain_table[0]
    )
    masked = pair_mask.astype(jnp.float32)[None]
    following, stored_first = block_forward(
        stream, masked, norm_gain[0], norm_shift[0], projections[0], output_weight[0], False
    )
    ignored, stored_second = block_forward(
        following.astype(jnp.float32),
        masked,
        norm_gain[1],
        norm_shift[1],
        projections[1],
        output_weight[1],
        True,
    )
    grad_mid, proj_second, out_second = block_backward(
        cotangent.astype(jnp.float32),
        stored_second,
        masked,
        norm_gain[1],
        projections[1],
        output_weight[1],
        True,
    )
    proj_second, out_second = reduce_block(proj_second, out_second)
    grad_first, proj_first, out_first = block_backward(
        grad_mid, stored_first, masked, norm_gain[0], projections[0], output_weight[0], False
    )
    proj_first, out_first = reduce_block(proj_first, out_first)
    scale_rows = 1.0 / residues
    projection_grads = jnp.stack([proj_first, proj_second]) * scale_rows
    weight_grad_out = jnp.stack([out_first, out_second]) * scale_rows
    return (grad_first.astype(jnp.bfloat16), projection_grads, weight_grad_out)


def solution(mesh):
    return jax.shard_map(
        shards,
        mesh=mesh,
        in_specs=(
            P(("groups", "dap"), None, None),
            P("groups"),
            P(("groups", "dap"), None),
            P(),
            P(),
            P(),
            P(),
            P(),
            P(("groups", "dap"), None, None),
        ),
        out_specs=(
            P(("groups", "dap"), None, None),
            P("groups", None, None, None),
            P("groups", None, None),
        ),
        check_vma=False,
    )
```

profile of v0, /device:TPU:0, one launch (start us, length us, event | category | flops | bytes accessed | tf_op | source)
XLA Modules:
  0.0 288.0 jit_solution(3440260031220799801)
XLA Ops:
  7.2 0.7 copy-done.54
  7.9 0.7 dynamic_slice.3
  8.6 0.7 broadcast_compare_fusion
  9.3 1.2 fusion.50
  10.9 0.7 copy-done.52
  12.2 1.3 convolution_bitcast_fusion.1
  14.8 0.7 copy.94
  15.5 7.4 %all-to-all-start.1 = ((bf16[16,8,5,80]{3,1,2,0:T(8,128)(2,1)}), bf16[16,8,5,80]{3,1,2,0:T(8,128)(2,1)S(1)}, u32[]{:S(2)}, u32[]{:S(2)}) async-start(bf16[16,8,5,80]{3,1,2,0:T(8,128)(2,1)} %copy.94), calls=%async_computation.1 | async-start | bytes 327680 | tf_op jit(solution)/shard_map/all_to_all | solution.py:68
  23.0 8.4 %all-to-all-done.1 = bf16[16,8,5,80]{3,1,2,0:T(8,128)(2,1)S(1)} async-done(((bf16[16,8,5,80]{3,1,2,0:T(8,128)(2,1)}), bf16[16,8,5,80]{3,1,2,0:T(8,128)(2,1)S(1)}, u32[]{:S(2)}, u32[]{:S(2)}) %all-to-all-start.1) | async-done | bytes 102432 | tf_op jit(solution)/shard_map/all_to_all | solution.py:68
  31.4 11.0 %all_to_all.144 = bf16[16,8,5,80]{3,1,2,0:T(8,128)(2,1)S(1)} all-to-all(bf16[16,8,5,80]{3,1,2,0:T(8,128)(2,1)S(1)} %copy.91), channel_id=1, replica_groups=mesh['groups'=2,'dap'=16] {'dap'}, dimensions={0} | all-to-all | bytes 204800 | tf_op jit(solution)/shard_map/all_to_all | solution.py:67
  42.7 0.7 copy.97
  43.4 3.5 %all-to-all-start.2 = ((bf16[1,8,80,80]{3,1,0,2:T(8,128)(2,1)}), bf16[1,8,80,80]{3,1,0,2:T(8,128)(2,1)S(1)}, u32[]{:S(2)}, u32[]{:S(2)}) async-start(bf16[1,8,80,80]{3,1,0,2:T(8,128)(2,1)} %copy.97), calls=%async_computation.2 | async-start | bytes 327680 | tf_op jit(solution)/shard_map/all_to_all | solution.py:71
  47.1 8.3 %all-to-all-done.2 = bf16[1,8,80,80]{3,1,0,2:T(8,128)(2,1)S(1)} async-done(((bf16[1,8,80,80]{3,1,0,2:T(8,128)(2,1)}), bf16[1,8,80,80]{3,1,0,2:T(8,128)(2,1)S(1)}, u32[]{:S(2)}, u32[]{:S(2)}) %all-to-all-start.2) | async-done | bytes 102432 | tf_op jit(solution)/shard_map/all_to_all | solution.py:71
  56.6 1.0 convert_reduce_fusion
  58.3 0.8 fusion.42
  59.4 1.1 copy.105
  60.5 1.8 copy.104
  62.4 1.7 fusion.20
  64.1 0.7 copy.106
  64.8 3.6 %all-to-all-start.4 = ((bf16[16,8,5,80]{3,1,2,0:T(8,128)(2,1)}), bf16[16,8,5,80]{3,1,2,0:T(8,128)(2,1)S(1)}, u32[]{:S(2)}, u32[]{:S(2)}) async-start(bf16[16,8,5,80]{3,1,2,0:T(8,128)(2,1)} %copy.106), calls=%async_computation.4 | async-start | bytes 327680 | tf_op jit(solution)/shard_map/all_to_all | solution.py:67
  68.5 0.7 add.175
  69.1 0.7 mul.492
  69.8 0.7 copy.103
  70.5 6.4 %all-to-all-done.4 = bf16[16,8,5,80]{3,1,2,0:T(8,128)(2,1)S(1)} async-done(((bf16[16,8,5,80]{3,1,2,0:T(8,128)(2,1)}), bf16[16,8,5,80]{3,1,2,0:T(8,128)(2,1)S(1)}, u32[]{:S(2)}, u32[]{:S(2)}) %all-to-all-start.4) | async-done | bytes 102432 | tf_op jit(solution)/shard_map/all_to_all | solution.py:67
  76.9 3.5 %all-to-all-start.3 = ((bf16[16,8,5,80]{3,1,2,0:T(8,128)(2,1)}), bf16[16,8,5,80]{3,1,2,0:T(8,128)(2,1)S(1)}, u32[]{:S(2)}, u32[]{:S(2)}) async-start(bf16[16,8,5,80]{3,1,2,0:T(8,128)(2,1)} %copy.103), calls=%async_computation.3 | async-start | bytes 327680 | tf_op jit(solution)/shard_map/all_to_all | solution.py:68
  80.6 8.2 %all-to-all-done.3 = bf16[16,8,5,80]{3,1,2,0:T(8,128)(2,1)S(1)} async-done(((bf16[16,8,5,80]{3,1,2,0:T(8,128)(2,1)}), bf16[16,8,5,80]{3,1,2,0:T(8,128)(2,1)S(1)}, u32[]{:S(2)}, u32[]{:S(2)}) %all-to-all-start.3) | async-done | bytes 102432 | tf_op jit(solution)/shard_map/all_to_all | solution.py:68
  89.1 0.7 copy.109
  89.8 3.5 %all-to-all-start.5 = ((bf16[1,8,80,80]{3,1,0,2:T(8,128)(2,1)}), bf16[1,8,80,80]{3,1,0,2:T(8,128)(2,1)S(1)}, u32[]{:S(2)}, u32[]{:S(2)}) async-start(bf16[1,8,80,80]{3,1,0,2:T(8,128)(2,1)} %copy.109), calls=%async_computation.5 | async-start | bytes 327680 | tf_op jit(solution)/shard_map/all_to_all | solution.py:71
  93.3 1.8 fusion.8
  95.1 6.6 %all-to-all-done.5 = bf16[1,8,80,80]{3,1,0,2:T(8,128)(2,1)S(1)} async-done(((bf16[1,8,80,80]{3,1,0,2:T(8,128)(2,1)}), bf16[1,8,80,80]{3,1,0,2:T(8,128)(2,1)S(1)}, u32[]{:S(2)}, u32[]{:S(2)}) %all-to-all-start.5) | async-done | bytes 102432 | tf_op jit(solution)/shard_map/all_to_all | solution.py:71
  102.1 0.7 copy-done.1
  102.8 1.4 fusion.116
  104.7 0.7 copy.114
  105.4 3.6 %all-to-all-start.6 = ((bf16[16,8,5,80]{3,1,2,0:T(8,128)(2,1)}), bf16[16,8,5,80]{3,1,2,0:T(8,128)(2,1)S(1)}, u32[]{:S(2)}, u32[]{:S(2)}) async-start(bf16[16,8,5,80]{3,1,2,0:T(8,128)(2,1)} %copy.114), calls=%async_computation.6 | async-start | bytes 327680 | tf_op jit(solution)/shard_map/all_to_all | solution.py:128
  109.1 1.8 fusion.18
  110.9 0.6 copy-done.41
  111.5 1.0 convolution_bitcast_fusion.6
  112.5 5.0 %all-to-all-done.6 = bf16[16,8,5,80]{3,1,2,0:T(8,128)(2,1)S(1)} async-done(((bf16[16,8,5,80]{3,1,2,0:T(8,128)(2,1)}), bf16[16,8,5,80]{3,1,2,0:T(8,128)(2,1)S(1)}, u32[]{:S(2)}, u32[]{:S(2)}) %all-to-all-start.6) | async-done | bytes 102432 | tf_op jit(solution)/shard_map/all_to_all | solution.py:128
  117.7 0.7 copy.117
  118.4 3.7 %all-to-all-start.7 = ((bf16[1,8,80,80]{3,1,0,2:T(8,128)(2,1)}), bf16[1,8,80,80]{3,1,0,2:T(8,128)(2,1)S(1)}, u32[]{:S(2)}, u32[]{:S(2)}) async-start(bf16[1,8,80,80]{3,1,0,2:T(8,128)(2,1)} %copy.117), calls=%async_computation.7 | async-start | bytes 327680 | tf_op jit(solution)/shard_map/all_to_all | solution.py:131
  122.1 1.0 convolution_bitcast_fusion.8
  123.4 0.7 copy.123
  124.1 6.5 %all-to-all-done.7 = bf16[1,8,80,80]{3,1,0,2:T(8,128)(2,1)S(1)} async-done(((bf16[1,8,80,80]{3,1,0,2:T(8,128)(2,1)}), bf16[1,8,80,80]{3,1,0,2:T(8,128)(2,1)S(1)}, u32[]{:S(2)}, u32[]{:S(2)}) %all-to-all-start.7) | async-done | bytes 102432 | tf_op jit(solution)/shard_map/all_to_all | solution.py:131
  130.5 3.5 %all-to-all-start.8 = ((bf16[1,8,80,80]{3,1,0,2:T(8,128)(2,1)}), bf16[1,8,80,80]{3,1,0,2:T(8,128)(2,1)S(1)}, u32[]{:S(2)}, u32[]{:S(2)}) async-start(bf16[1,8,80,80]{3,1,0,2:T(8,128)(2,1)} %copy.123), calls=%async_computation.8 | async-start | bytes 327680 | tf_op jit(solution)/shard_map/all_to_all | solution.py:132
  134.2 8.2 %all-to-all-done.8 = bf16[1,8,80,80]{3,1,0,2:T(8,128)(2,1)S(1)} async-done(((bf16[1,8,80,80]{3,1,0,2:T(8,128)(2,1)}), bf16[1,8,80,80]{3,1,0,2:T(8,128)(2,1)S(1)}, u32[]{:S(2)}, u32[]{:S(2)}) %all-to-all-start.8) | async-done | bytes 102432 | tf_op jit(solution)/shard_map/all_to_all | solution.py:132
  142.9 0.7 copy-done.5
  147.4 0.7 copy.132
  148.1 3.7 %all-to-all-start.9 = ((bf16[16,8,5,80]{3,1,2,0:T(8,128)(2,1)}), bf16[16,8,5,80]{3,1,2,0:T(8,128)(2,1)S(1)}, u32[]{:S(2)}, u32[]{:S(2)}) async-start(bf16[16,8,5,80]{3,1,2,0:T(8,128)(2,1)} %copy.132), calls=%async_computation.9 | async-start | bytes 327680 | tf_op jit(solution)/shard_map/all_to_all | solution.py:128
  151.8 0.7 copy-done.50
  152.5 1.0 convolution_bitcast_fusion.7
  155.5 4.5 %all-to-all-done.9 = bf16[16,8,5,80]{3,1,2,0:T(8,128)(2,1)S(1)} async-done(((bf16[16,8,5,80]{3,1,2,0:T(8,128)(2,1)}), bf16[16,8,5,80]{3,1,2,0:T(8,128)(2,1)S(1)}, u32[]{:S(2)}, u32[]{:S(2)}) %all-to-all-start.9) | async-done | bytes 102432 | tf_op jit(solution)/shard_map/all_to_all | solution.py:128
  160.5 0.7 copy.135
  161.2 3.6 %all-to-all-start.10 = ((bf16[1,8,80,80]{3,1,0,2:T(8,128)(2,1)}), bf16[1,8,80,80]{3,1,0,2:T(8,128)(2,1)S(1)}, u32[]{:S(2)}, u32[]{:S(2)}) async-start(bf16[1,8,80,80]{3,1,0,2:T(8,128)(2,1)} %copy.135), calls=%async_computation.10 | async-start | bytes 327680 | tf_op jit(solution)/shard_map/all_to_all | solution.py:131
  164.8 0.7 maximum_bitcast_fusion.1
  165.8 0.7 copy.141
  166.5 6.7 %all-to-all-done.10 = bf16[1,8,80,80]{3,1,0,2:T(8,128)(2,1)S(1)} async-done(((bf16[1,8,80,80]{3,1,0,2:T(8,128)(2,1)}), bf16[1,8,80,80]{3,1,0,2:T(8,128)(2,1)S(1)}, u32[]{:S(2)}, u32[]{:S(2)}) %all-to-all-start.10) | async-done | bytes 102432 | tf_op jit(solution)/shard_map/all_to_all | solution.py:131
  173.2 3.5 %all-to-all-start.11 = ((bf16[1,8,80,80]{3,1,0,2:T(8,128)(2,1)}), bf16[1,8,80,80]{3,1,0,2:T(8,128)(2,1)S(1)}, u32[]{:S(2)}, u32[]{:S(2)}) async-start(bf16[1,8,80,80]{3,1,0,2:T(8,128)(2,1)} %copy.141), calls=%async_computation.11 | async-start | bytes 327680 | tf_op jit(solution)/shard_map/all_to_all | solution.py:132
  177.0 8.2 %all-to-all-done.11 = bf16[1,8,80,80]{3,1,0,2:T(8,128)(2,1)S(1)} async-done(((bf16[1,8,80,80]{3,1,0,2:T(8,128)(2,1)}), bf16[1,8,80,80]{3,1,0,2:T(8,128)(2,1)S(1)}, u32[]{:S(2)}, u32[]{:S(2)}) %all-to-all-start.11) | async-done | bytes 102432 | tf_op jit(solution)/shard_map/all_to_all | solution.py:132
  186.9 0.8 maximum_bitcast_fusion
  187.7 1.2 add_convert_fusion.4
  188.9 89.4 %all-reduce.3.cloned.1.call-done = (f32[1,5,128,128]{2,3,1,0:T(8,128)}, f32[1,5,128,128]{2,3,1,0:T(8,128)}, f32[1,128,128]{2,1,0:T(8,128)}, f32[1,128,128]{2,1,0:T(8,128)}) async-done(((f32[1,5,128,128]{2,3,1,0:T(8,128)}, f32[1,5,128,128]{2,3,1,0:T(8,128)}, f32[1,128,128]{2,1,0:T(8,128)}, f32[1,128,128]{2,1,0:T(8,128)}), (f32[1,5,128,128]{2,3,1,0:T(8,128)}, f32[1,5,128,128]{2,3,1,0:T(8,128)}, ...) | async-done | bytes 786448 | tf_op jit(solution)/shard_map/psum | solution.py:164
  278.3 1.1 maximum_multiply_fusion
  279.4 1.1 copy.147
  280.5 0.7 maximum_multiply_fusion.1
  (178 shorter events, 15.4 us)
Async XLA Ops:
  7.2 0.7 copy-start.54
  7.2 3.3 %copy-start = (bf16[5,80,128]{2,1,0:T(8,128)(2,1)S(1)}, bf16[5,80,128]{2,1,0:T(8,128)(2,1)}, u32[]{:S(2)}) copy-start(bf16[5,80,128]{2,1,0:T(8,128)(2,1)} %param.9) | copy-start | bytes 307204
  7.8 48.7 %copy-start.32 = (f32[128]{0:T(128)}, f32[128]{0:T(128)S(1)}, u32[]{:S(2)}) copy-start(f32[128]{0:T(128)S(1)} %get-tuple-element.66) | copy-start | bytes 1540
  7.9 48.7 %copy-start.34 = (f32[128]{0:T(128)}, f32[128]{0:T(128)S(1)}, u32[]{:S(2)}) copy-start(f32[128]{0:T(128)S(1)} %get-tuple-element.67) | copy-start | bytes 1540
  9.3 47.3 %copy-start.30 = (pred[5,80]{1,0:T(8,128)(4,1)}, pred[5,80]{1,0:T(8,128)(4,1)S(1)}, u32[]{:S(2)}) copy-start(pred[5,80]{1,0:T(8,128)(4,1)S(1)} %broadcast_compare_fusion) | copy-start | bytes 1204
  10.5 46.1 %copy-start.26 = (f32[5,80]{1,0:T(8,128)}, f32[5,80]{1,0:T(8,128)S(1)}, u32[]{:S(2)}) copy-start(f32[5,80]{1,0:T(8,128)S(1)} %broadcast_multiply_fusion.11) | copy-start | bytes 4804
  10.8 0.7 copy-start.52
  10.8 0.7 copy-start.53
  11.5 45.1 %copy-start.28 = (f32[5,80]{1,0:T(8,128)}, f32[5,80]{1,0:T(8,128)S(1)}, u32[]{:S(2)}) copy-start(f32[5,80]{1,0:T(8,128)S(1)} %add_rsqrt_fusion.3) | copy-start | bytes 4804
  12.1 44.5 %copy-start.43 = (f32[128]{0:T(128)}, f32[128]{0:T(128)S(1)}, u32[]{:S(2)}) copy-start(f32[128]{0:T(128)S(1)} %get-tuple-element.65) | copy-start | bytes 1540
  12.1 44.5 %copy-start.45 = (f32[128]{0:T(128)}, f32[128]{0:T(128)S(1)}, u32[]{:S(2)}) copy-start(f32[128]{0:T(128)S(1)} %get-tuple-element.76) | copy-start | bytes 1540
  12.1 81.2 %copy-start.36 = (f32[128]{0:T(128)}, f32[128]{0:T(128)S(1)}, u32[]{:S(2)}) copy-start(f32[128]{0:T(128)S(1)} %get-tuple-element.64) | copy-start | bytes 1540
  12.1 81.2 %copy-start.47 = (f32[128]{0:T(128)}, f32[128]{0:T(128)S(1)}, u32[]{:S(2)}) copy-start(f32[128]{0:T(128)S(1)} %get-tuple-element.73) | copy-start | bytes 1540
  12.1 90.0 %copy-start.40 = (f32[128]{0:T(128)}, f32[128]{0:T(128)S(1)}, u32[]{:S(2)}) copy-start(f32[128]{0:T(128)S(1)} %get-tuple-element.63) | copy-start | bytes 1540
  13.7 0.7 copy-start.42
  15.5 15.9 %all-to-all-start.1 = ((bf16[16,8,5,80]{3,1,2,0:T(8,128)(2,1)}), bf16[16,8,5,80]{3,1,2,0:T(8,128)(2,1)S(1)}, u32[]{:S(2)}, u32[]{:S(2)}) async-start(bf16[16,8,5,80]{3,1,2,0:T(8,128)(2,1)} %copy.94), calls=%async_computation.1 | async-start | bytes 327680 | tf_op jit(solution)/shard_map/all_to_all | solution.py:68
  43.4 12.0 %all-to-all-start.2 = ((bf16[1,8,80,80]{3,1,0,2:T(8,128)(2,1)}), bf16[1,8,80,80]{3,1,0,2:T(8,128)(2,1)S(1)}, u32[]{:S(2)}, u32[]{:S(2)}) async-start(bf16[1,8,80,80]{3,1,0,2:T(8,128)(2,1)} %copy.97), calls=%async_computation.2 | async-start | bytes 327680 | tf_op jit(solution)/shard_map/all_to_all | solution.py:71
  55.4 0.8 copy-start.24
  55.5 1.1 copy-start.4
  56.6 1.1 copy-start.6
  58.0 35.4 %copy-start.13 = (f32[5,80]{1,0:T(8,128)}, f32[5,80]{1,0:T(8,128)S(1)}, u32[]{:S(2)}) copy-start(f32[5,80]{1,0:T(8,128)S(1)} %add_rsqrt_fusion.1) | copy-start | bytes 4804
  64.8 5.0 %copy-start.3 = (bf16[16,8,5,80]{3,1,0,2:T(8,128)(2,1)S(1)}, bf16[16,8,5,80]{3,1,0,2:T(8,128)(2,1)}, u32[]{:S(2)}) copy-start(bf16[16,8,5,80]{3,1,0,2:T(8,128)(2,1)} %get-tuple-element.52) | copy-start | bytes 307204
  64.8 12.1 %all-to-all-start.4 = ((bf16[16,8,5,80]{3,1,2,0:T(8,128)(2,1)}), bf16[16,8,5,80]{3,1,2,0:T(8,128)(2,1)S(1)}, u32[]{:S(2)}, u32[]{:S(2)}) async-start(bf16[16,8,5,80]{3,1,2,0:T(8,128)(2,1)} %copy.106), calls=%async_computation.4 | async-start | bytes 327680 | tf_op jit(solution)/shard_map/all_to_all | solution.py:67
  76.9 11.9 %all-to-all-start.3 = ((bf16[16,8,5,80]{3,1,2,0:T(8,128)(2,1)}), bf16[16,8,5,80]{3,1,2,0:T(8,128)(2,1)S(1)}, u32[]{:S(2)}, u32[]{:S(2)}) async-start(bf16[16,8,5,80]{3,1,2,0:T(8,128)(2,1)} %copy.103), calls=%async_computation.3 | async-start | bytes 327680 | tf_op jit(solution)/shard_map/all_to_all | solution.py:68
  89.8 11.9 %all-to-all-start.5 = ((bf16[1,8,80,80]{3,1,0,2:T(8,128)(2,1)}), bf16[1,8,80,80]{3,1,0,2:T(8,128)(2,1)S(1)}, u32[]{:S(2)}, u32[]{:S(2)}) async-start(bf16[1,8,80,80]{3,1,0,2:T(8,128)(2,1)} %copy.109), calls=%async_computation.5 | async-start | bytes 327680 | tf_op jit(solution)/shard_map/all_to_all | solution.py:71
  101.8 2.4 copy-start.9
  101.9 2.3 copy-start.19
  101.9 0.9 copy-start.1
  105.4 3.7 %copy-start.2 = (f32[5,80,128]{2,1,0:T(8,128)S(1)}, f32[5,80,128]{2,1,0:T(8,128)}, u32[]{:S(2)}) copy-start(f32[5,80,128]{2,1,0:T(8,128)} %fusion.8) | copy-start | bytes 614404
  105.4 12.1 %all-to-all-start.6 = ((bf16[16,8,5,80]{3,1,2,0:T(8,128)(2,1)}), bf16[16,8,5,80]{3,1,2,0:T(8,128)(2,1)S(1)}, u32[]{:S(2)}, u32[]{:S(2)}) async-start(bf16[16,8,5,80]{3,1,2,0:T(8,128)(2,1)} %copy.114), calls=%async_computation.6 | async-start | bytes 327680 | tf_op jit(solution)/shard_map/all_to_all | solution.py:128
  109.1 1.8 copy-start.10
  109.1 1.8 copy-start.20
  110.9 0.7 copy-start.51
  118.4 3.7 %copy-start.14 = (f32[5,80]{1,0:T(8,128)S(1)}, f32[5,80]{1,0:T(8,128)}, u32[]{:S(2)}) copy-start(f32[5,80]{1,0:T(8,128)} %copy-done.13) | copy-start | bytes 4804
  118.4 3.7 %copy-start.15 = (bf16[5,80,128]{2,1,0:T(8,128)(2,1)S(1)}, bf16[5,80,128]{2,1,0:T(8,128)(2,1)}, u32[]{:S(2)}) copy-start(bf16[5,80,128]{2,1,0:T(8,128)(2,1)} %fusion.18) | copy-start | bytes 307204
  118.4 3.7 %copy-start.37 = (f32[128]{0:T(128)S(1)}, f32[128]{0:T(128)}, u32[]{:S(2)}) copy-start(f32[128]{0:T(128)} %copy-done.36) | copy-start | bytes 1540
  118.4 3.7 %copy-start.48 = (f32[128]{0:T(128)S(1)}, f32[128]{0:T(128)}, u32[]{:S(2)}) copy-start(f32[128]{0:T(128)} %copy-done.47) | copy-start | bytes 1540
  118.4 12.1 %all-to-all-start.7 = ((bf16[1,8,80,80]{3,1,0,2:T(8,128)(2,1)}), bf16[1,8,80,80]{3,1,0,2:T(8,128)(2,1)S(1)}, u32[]{:S(2)}, u32[]{:S(2)}) async-start(bf16[1,8,80,80]{3,1,0,2:T(8,128)(2,1)} %copy.117), calls=%async_computation.7 | async-start | bytes 327680 | tf_op jit(solution)/shard_map/all_to_all | solution.py:131
  130.5 11.9 %all-to-all-start.8 = ((bf16[1,8,80,80]{3,1,0,2:T(8,128)(2,1)}), bf16[1,8,80,80]{3,1,0,2:T(8,128)(2,1)S(1)}, u32[]{:S(2)}, u32[]{:S(2)}) async-start(bf16[1,8,80,80]{3,1,0,2:T(8,128)(2,1)} %copy.123), calls=%async_computation.8 | async-start | bytes 327680 | tf_op jit(solution)/shard_map/all_to_all | solution.py:132
  142.6 1.0 copy-start.5
  142.9 1.0 copy-start.11
  143.6 0.9 copy-start.16
  144.5 0.9 copy-start.7
  144.5 1.0 copy-start.8
  145.6 0.7 copy-start.18
  145.6 0.8 copy-start.25
  148.1 12.0 %all-to-all-start.9 = ((bf16[16,8,5,80]{3,1,2,0:T(8,128)(2,1)}), bf16[16,8,5,80]{3,1,2,0:T(8,128)(2,1)S(1)}, u32[]{:S(2)}, u32[]{:S(2)}) async-start(bf16[16,8,5,80]{3,1,2,0:T(8,128)(2,1)} %copy.132), calls=%async_computation.9 | async-start | bytes 327680 | tf_op jit(solution)/shard_map/all_to_all | solution.py:128
  151.8 0.7 copy-start.50
  152.5 1.0 copy-start.27
  152.5 1.0 copy-start.29
  152.5 1.0 copy-start.35
  152.5 1.0 copy-start.44
  152.5 1.0 copy-start.46
  153.5 0.7 copy-start.31
  153.5 0.7 copy-start.33
  154.1 0.9 copy-start.12
  154.1 0.9 copy-start.38
  154.1 0.9 copy-start.49
  161.2 3.7 %copy-start.21 = (f32[1,128,128]{1,2,0:T(8,128)S(1)}, f32[1,128,128]{1,2,0:T(8,128)}, u32[]{:S(2)}) copy-start(f32[1,128,128]{1,2,0:T(8,128)} %convolution_bitcast_fusion.8) | copy-start | bytes 196612
  161.2 12.1 %all-to-all-start.10 = ((bf16[1,8,80,80]{3,1,0,2:T(8,128)(2,1)}), bf16[1,8,80,80]{3,1,0,2:T(8,128)(2,1)S(1)}, u32[]{:S(2)}, u32[]{:S(2)}) async-start(bf16[1,8,80,80]{3,1,0,2:T(8,128)(2,1)} %copy.135), calls=%async_computation.10 | async-start | bytes 327680 | tf_op jit(solution)/shard_map/all_to_all | solution.py:131
  173.2 11.9 %all-to-all-start.11 = ((bf16[1,8,80,80]{3,1,0,2:T(8,128)(2,1)}), bf16[1,8,80,80]{3,1,0,2:T(8,128)(2,1)S(1)}, u32[]{:S(2)}, u32[]{:S(2)}) async-start(bf16[1,8,80,80]{3,1,0,2:T(8,128)(2,1)} %copy.141), calls=%async_computation.11 | async-start | bytes 327680 | tf_op jit(solution)/shard_map/all_to_all | solution.py:132
  176.8 101.5 %all-reduce.3.cloned.1.call-start = ((), (), s32[]{:S(2)}) async-start(), calls=%async_computation.12 | async-start | bytes 1572864 | tf_op jit(solution)/shard_map/psum | solution.py:164
  279.4 1.1 copy-start.22
  279.4 1.1 copy-start.23
  (3 other events, 1.9 us)
Sparse Core Ops, SparseCore 0:
  187.8 90.4 all-reduce.2
where the time goes:
time: 290 us; the launch traced here: 288 us
  waiting for transfers between devices  166 us (57%)
  starting transfers between devices  43.3 us (15%)
  local copies, waits for them, and re-layouts  25.5 us (9%)
  matrix products  15.4 us (5%)
  between operations  14.9 us (5%)
  other arithmetic  11.5 us (4%)
  blocking collectives  11 us (4%)
    psum x1, waiting for transfers between devices, reduce_block(): return lax.psum((weight_grads, out_weight_grad), 'dap')  89.4 us
    all_to_all x2, waiting for transfers between devices, block_forward(): lax.all_to_all(right_blocks, 'dap', split_axis=0, concat_axis=2, tiled=True)  16.7 us
    all_to_all x2, waiting for transfers between devices, block_backward(): lax.all_to_all(right_grad, 'dap', split_axis=2, concat_axis=0, tiled=True)  16.4 us
    all_to_all x2, waiting for transfers between devices, block_forward(): lax.all_to_all(product, 'dap', split_axis=2, concat_axis=0, tiled=True)  14.9 us
    all_to_all x2, waiting for transfers between devices, block_backward(): lax.all_to_all(left_grad, 'dap', split_axis=2, concat_axis=0, tiled=True)  13.2 us
    all_to_all x1, blocking collectives, block_forward(): lax.all_to_all(left_blocks, 'dap', split_axis=0, concat_axis=2, tiled=True)  11 us
    all_to_all x2, starting transfers between devices, block_forward(): lax.all_to_all(right_blocks, 'dap', split_axis=0, concat_axis=2, tiled=True)  10.9 us
    unnamed x111, local copies, waits for them, and re-layouts  9.48 us
  transfers between devices with their start and end apart: 12, of which 12 were waited for; matrix products, arithmetic and copies ran while one was open for 5% of the time, Pallas kernels for 0%

commit v1 on v0

--- a/solution.py
+++ b/solution.py
@@ -1,6 +1,10 @@
+import functools
+
 import jax
 import jax.numpy as jnp
 from jax import lax
+from jax.experimental import pallas as pl
+from jax.experimental.pallas import tpu as pltpu
 from jax.sharding import PartitionSpec as P
 
 EPSILON = 1e-05
@@ -164,7 +168,7 @@
     return lax.psum((weight_grads, out_weight_grad), "dap")
 
 
-def shards(
+def sharded_ops(
     pair_state,
     chain_index,
     pair_mask,
@@ -213,6 +217,488 @@
     projection_grads = jnp.stack([proj_first, proj_second]) * scale_rows
     weight_grad_out = jnp.stack([out_first, out_second]) * scale_rows
     return (grad_first.astype(jnp.bfloat16), projection_grads, weight_grad_out)
+
+
+LANES = 128
+F32 = jnp.float32
+BF16 = jnp.bfloat16
+
+
+def dot(left, right, left_dim, right_dim):
+    return lax.dot_general(
+        left, right, (((left_dim,), (right_dim,)), ((), ())), preferred_element_type=F32
+    )
+
+
+def norm_lanes(values):
+    center = values - jnp.mean(values, axis=1, keepdims=True)
+    inverse = lax.rsqrt(jnp.mean(center * center, axis=1, keepdims=True) + EPSILON)
+    return center * inverse, inverse
+
+
+def norm_lanes_back(grad, normed, inverse, gain):
+    scaled = grad * gain
+    centered = scaled - jnp.mean(scaled, axis=1, keepdims=True)
+    return (centered - normed * jnp.mean(scaled * normed, axis=1, keepdims=True)) * inverse
+
+
+def fused_kernel(
+    n,
+    rows,
+    residues,
+    pair_ref,
+    chain_ref,
+    mask_ref,
+    table_ref,
+    gain_ref,
+    shift_ref,
+    proj_ref,
+    weight_ref,
+    cot_ref,
+    grad_out,
+    proj_out,
+    weight_out,
+    stream,
+    mask,
+    normed_in,
+    inverse_in,
+    normed_out,
+    inverse_out,
+    activated,
+    pre,
+    mixture,
+    update,
+    up,
+    mix_grad,
+    update_grad,
+    pre_grad,
+    factors,
+    stage16,
+    stage8,
+    rows16,
+    rows8,
+    wide_send,
+    wide_recv,
+    thin_send,
+    thin_recv,
+    sum_send,
+    sum_recv,
+    all_send,
+    all_recv,
+    total,
+    send_sem,
+    recv_sem,
+):
+    channels = LANES
+    slices = channels // n
+    padded = factors.shape[-1]
+    pairs = rows * residues
+    share = sum_recv.shape[2]
+    double = 2 * slices
+    me = lax.axis_index("dap")
+    barrier = pltpu.get_barrier_semaphore()
+
+    def each_peer(body):
+        def step(index, carry):
+            body(lax.rem(me + index, n))
+            return carry
+
+        lax.fori_loop(1, n, step, 0)
+
+    def greet(peer):
+        pl.semaphore_signal(
+            barrier, inc=1, device_id={"dap": peer}, device_id_type=pl.DeviceIdType.MESH
+        )
+
+    each_peer(greet)
+
+    def copy(phase, source, target, peer, owner):
+        return pltpu.make_async_remote_copy(
+            src_ref=source,
+            dst_ref=target.at[owner],
+            send_sem=send_sem.at[phase, peer],
+            recv_sem=recv_sem.at[phase, owner],
+            device_id={"dap": peer},
+            device_id_type=pl.DeviceIdType.MESH,
+        )
+
+    def send_all(phase, source_of, target):
+        target[me] = source_of(me)[...]
+        each_peer(lambda peer: copy(phase, source_of(peer), target, peer, me).start())
+
+    def take_all(phase, source_of, target):
+        each_peer(lambda peer: copy(phase, source_of(peer), target, peer, peer).wait_recv())
+
+    def end_all(phase, source_of, target):
+        each_peer(lambda peer: copy(phase, source_of(peer), target, peer, me).wait_send())
+
+    def span(row):
+        return pl.ds(row * residues, residues)
+
+    def to_columns(values):
+        filler = jnp.zeros((padded - residues, channels), F32)
+        full = jnp.concatenate([values, filler], axis=0) if padded > residues else values
+        return full.T.reshape(n, slices, padded)
+
+    def to_rows(blocks):
+        return blocks.reshape(channels, padded).T[:residues]
+
+    def wide(number):
+        return lambda peer: wide_send.at[number, peer]
+
+    def thin(number):
+        return lambda peer: thin_send.at[number, peer]
+
+    def shares(number):
+        return lambda peer: sum_send.at[
+            number, pl.ds(pl.multiple_of(peer * share, 16), share)
+        ]
+
+    def whole_share(number):
+        return lambda peer: all_send.at[number]
+
+    exchanges = {
+        0: (wide(0), wide_recv.at[0]),
+        1: (thin(0), thin_recv.at[0]),
+        2: (wide(1), wide_recv.at[1]),
+        3: (thin(1), thin_recv.at[1]),
+        4: (thin(2), thin_recv.at[2]),
+        5: (wide(2), wide_recv.at[2]),
+        6: (thin(3), thin_recv.at[3]),
+        7: (wide(3), wide_recv.at[3]),
+        8: (shares(1), sum_recv.at[1]),
+        9: (whole_share(1), all_recv.at[1]),
+        10: (shares(0), sum_recv.at[0]),
+        11: (whole_share(0), all_recv.at[0]),
+    }
+
+    stage16[...] = jnp.zeros_like(stage16)
+    stage8[...] = jnp.zeros_like(stage8)
+    rows8[...] = jnp.zeros_like(rows8)
+
+    chain = chain_ref[...]
+    place = lax.broadcasted_iota(jnp.int32, chain.shape, 1)
+    for row in range(rows):
+        own = jnp.sum(jnp.where(place == me * rows + row, chain, 0), axis=1, keepdims=True)
+        same = jnp.where(chain == own, 1.0, 0.0).astype(F32)
+        filler = jnp.zeros((1, padded - residues), F32)
+        seen = mask_ref[pl.ds(row, 1), :].astype(F32)
+        if padded > residues:
+            same = jnp.concatenate([same, filler], axis=1)
+            seen = jnp.concatenate([seen, filler], axis=1)
+        same = jnp.broadcast_to(same, (channels, padded)).T[:residues]
+        mask[span(row), :] = jnp.broadcast_to(seen, (channels, padded)).T[:residues]
+        stream[0, span(row), :] = pair_ref[row].astype(F32) + jnp.where(
+            same > 0.5, table_ref[1:2, :], table_ref[0:1, :]
+        )
+
+    def send_factors(number):
+        gain, shift = gain_ref[number, 0:1, :], shift_ref[number, 0:1, :]
+        for row in range(rows):
+            normed, inverse = norm_lanes(stream[number, span(row), :])
+            normed_in[number, span(row), :] = normed
+            inverse_in[number, span(row), :] = jnp.broadcast_to(inverse, normed.shape)
+            activated[number, span(row), :] = (normed * gain + shift).astype(BF16)
+        for part in range(5):
+            pre[number, part] = dot(activated[number], proj_ref[number, part], 1, 0)
+        for row in range(rows):
+            seen = mask[span(row), :]
+            left = seen * jax.nn.sigmoid(pre[number, 1, span(row)]) * pre[number, 0, span(row)]
+            right = seen * jax.nn.sigmoid(pre[number, 3, span(row)]) * pre[number, 2, span(row)]
+            both = jnp.concatenate([to_columns(left), to_columns(right)], axis=1)
+            wide_send[number, :, pl.ds(row * double, double), :] = both.astype(BF16)
+        if number == 0:
+            pl.semaphore_wait(barrier, n - 1)
+        send_all(2 * number, *exchanges[2 * number])
+
+    def send_product(number):
+        take_all(2 * number, *exchanges[2 * number])
+        for owner in range(n):
+            stage16[pl.ds(owner * rows * double, rows * double), :] = wide_recv[
+                number, owner
+            ].astype(F32)
+        for channel in range(slices):
+            left = stage16[pl.ds(channel, padded, stride=double), :].astype(BF16)
+            right = stage16[pl.ds(slices + channel, padded, stride=double), :].astype(BF16)
+            factors[number, 0, channel] = left
+            factors[number, 1, channel] = right
+            stage8[pl.ds(channel, padded, stride=slices), :] = dot(
+                left, right, 1 - number, 1 - number
+            )
+        thin_rows = thin_send.shape[2]
+        for owner in range(n):
+            thin_send[number, owner] = stage8[
+                pl.ds(owner * rows * slices, thin_rows), :
+            ].astype(BF16)
+        send_all(2 * number + 1, *exchanges[2 * number + 1])
+
+    def take_product(number):
+        take_all(2 * number + 1, *exchanges[2 * number + 1])
+        gain, shift = gain_ref[number, 1:2, :], shift_ref[number, 1:2, :]
+        rows8[...] = thin_recv[number].astype(F32)
+        for row in range(rows):
+            product = to_rows(rows8[:, pl.ds(row * slices, slices), :])
+            normed, inverse = norm_lanes(product)
+            normed_out[number, span(row), :] = normed
+            inverse_out[number, span(row), :] = jnp.broadcast_to(inverse, normed.shape)
+            mixture[number, span(row), :] = (normed * gain + shift).astype(BF16)
+
+    def take_update(number):
+        update[number] = dot(mixture[number], weight_ref[number], 1, 0)
+
+    def mixture_back(number):
+        for row in range(rows):
+            gate = jax.nn.sigmoid(pre[number, 4, span(row)])
+            update_grad[number, span(row), :] = (up[number, span(row)] * gate).astype(BF16)
+        mix_grad[...] = dot(update_grad[number], weight_ref[number], 1, 1)
+
+    def send_product_grad(number):
+        gain = gain_ref[number, 1:2, :]
+        for row in range(rows):
+            grad = norm_lanes_back(
+                mix_grad[span(row), :],
+                normed_out[number, span(row), :],
+                inverse_out[number, span(row), :],
+                gain,
+            )
+            rows8[:, pl.ds(row * slices, slices), :] = to_columns(grad)
+        thin_send[3 - number] = rows8[...].astype(BF16)
+        send_all(6 - 2 * number, *exchanges[6 - 2 * number])
+
+    def gate_back(number):
+        for row in range(rows):
+            gate = jax.nn.sigmoid(pre[number, 4, span(row)])
+            pre_grad[number, 4, span(row), :] = (
+                up[number, span(row)] * update[number, span(row)] * gate * (1.0 - gate)
+            ).astype(BF16)
+
+    def weight_sum(number, part):
+        if part == 5:
+            grad = dot(mixture[number], update_grad[number], 0, 0)
+        else:
+            grad = dot(activated[number], pre_grad[number, part], 0, 0)
+        sum_send[number, pl.ds(part * channels, channels), :] = (
+            grad * (1.0 / residues)
+        ).astype(BF16)
+
+    def send_factor_grads(number):
+        phase = 6 - 2 * number
+        take_all(phase, *exchanges[phase])
+        for owner in range(n):
+            block = thin_recv[3 - number, owner].astype(F32)
+            stage8[pl.ds(owner * rows * slices, rows * slices), :] = block[: rows * slices]
+        if padded > residues:
+            stage8[pl.ds(residues * slices, (padded - residues) * slices), :] = jnp.zeros(
+                ((padded - residues) * slices, padded), F32
+            )
+        for channel in range(slices):
+            grad = stage8[pl.ds(channel, padded, stride=slices), :].astype(BF16)
+            left, right = factors[number, 0, channel], factors[number, 1, channel]
+            if number == 0:
+                left_grad = dot(grad, right, 1, 0)
+                right_grad = dot(grad, left, 0, 0)
+            else:
+                left_grad = dot(right, grad, 1, 1)
+                right_grad = dot(left, grad, 1, 0)
+            stage16[pl.ds(channel, padded, stride=double), :] = left_grad
+            stage16[pl.ds(slices + channel, padded, stride=double), :] = right_grad
+        for owner in range(n):
+            wide_send[3 - number, owner] = stage16[
+                pl.ds(owner * rows * double, rows * double), :
+            ].astype(BF16)
+        send_all(phase + 1, *exchanges[phase + 1])
+
+    def take_factor_grads(number):
+        phase = 7 - 2 * number
+        take_all(phase, *exchanges[phase])
+        rows16[...] = wide_recv[3 - number].astype(F32)
+        for row in range(rows):
+            seen = mask[span(row), :]
+            for side in range(2):
+                grad = seen * to_rows(rows16[:, pl.ds(row * double + side * slices, slices), :])
+                gate = jax.nn.sigmoid(pre[number, 2 * side + 1, span(row)])
+                opened = grad * gate
+                pre_grad[number, 2 * side, span(row), :] = opened.astype(BF16)
+                pre_grad[number, 2 * side + 1, span(row), :] = (
+                    opened * pre[number, 2 * side, span(row)] * (1.0 - gate)
+                ).astype(BF16)
+
+    def stream_back(number):
+        inner = dot(pre_grad[number, 0], proj_ref[number, 0], 1, 1)
+        for part in range(1, 5):
+            inner = inner + dot(pre_grad[number, part], proj_ref[number, part], 1, 1)
+        mix_grad[...] = inner
+        gain = gain_ref[number, 0:1, :]
+        for row in range(rows):
+            grad = up[number, span(row)] + norm_lanes_back(
+                mix_grad[span(row), :],
+                normed_in[number, span(row), :],
+                inverse_in[number, span(row), :],
+                gain,
+            )
+            if number == 1:
+                up[0, span(row), :] = grad
+            else:
+                grad_out[row] = grad.astype(BF16)
+
+    def send_total(number):
+        phase = 10 - 2 * number
+        take_all(phase, *exchanges[phase])
+        result = sum_recv[number, 0].astype(F32)
+        for owner in range(1, n):
+            result = result + sum_recv[number, owner].astype(F32)
+        all_send[number] = result.astype(BF16)
+        send_all(phase + 1, *exchanges[phase + 1])
+
+    def take_total(number):
+        phase = 11 - 2 * number
+        take_all(phase, *exchanges[phase])
+        for owner in range(n):
+            total[pl.ds(owner * share, share), :] = all_recv[number, owner].astype(F32)
+        for part in range(5):
+            proj_out[number, part] = total[pl.ds(part * channels, channels), :]
+        weight_out[number] = total[pl.ds(5 * channels, channels), :]
+
+    send_factors(0)
+    up[1] = cot_ref[...].reshape(pairs, channels).astype(F32)
+    send_product(0)
+    take_product(0)
+    take_update(0)
+    for row in range(rows):
+        gate = jax.nn.sigmoid(pre[0, 4, span(row)])
+        stream[1, span(row), :] = (
+            (stream[0, span(row), :] + gate * update[0, span(row)]).astype(BF16).astype(F32)
+        )
+    send_factors(1)
+    mixture_back(1)
+    send_product(1)
+    take_product(1)
+    send_product_grad(1)
+    take_update(1)
+    gate_back(1)
+    send_factor_grads(1)
+    weight_sum(1, 4)
+    weight_sum(1, 5)
+    take_factor_grads(1)
+    stream_back(1)
+    mixture_back(0)
+    send_product_grad(0)
+    for part in range(4):
+        weight_sum(1, part)
+    send_all(8, *exchanges[8])
+    gate_back(0)
+    send_factor_grads(0)
+    weight_sum(0, 4)
+    weight_sum(0, 5)
+    send_total(1)
+    take_factor_grads(0)
+    for part in range(4):
+        weight_sum(0, part)
+    send_all(10, *exchanges[10])
+    stream_back(0)
+    take_total(1)
+    send_total(0)
+    take_total(0)
+    for phase in range(12):
+        end_all(phase, *exchanges[phase])
+
+
+def fused(
+    pair_state,
+    chain_index,
+    pair_mask,
+    chain_table,
+    norm_gain,
+    norm_shift,
+    projections,
+    output_weight,
+    cotangent,
+):
+    rows, residues, channels = pair_state.shape
+    n = lax.axis_size("dap")
+    slices = channels // n
+    padded = -(-residues // LANES) * LANES
+    pairs = rows * residues
+    double = rows * 2 * slices
+    single = -(-rows * slices // 16) * 16
+    share = 6 * channels // n
+    vmem = pl.BlockSpec(memory_space=pltpu.VMEM)
+    return pl.pallas_call(
+        functools.partial(fused_kernel, n, rows, residues),
+        out_shape=(
+            jax.ShapeDtypeStruct((rows, residues, channels), BF16),
+            jax.ShapeDtypeStruct((2, 5, channels, channels), F32),
+            jax.ShapeDtypeStruct((2, channels, channels), F32),
+        ),
+        in_specs=[vmem] * 9,
+        out_specs=(vmem,) * 3,
+        scratch_shapes=[
+            pltpu.VMEM((2, pairs, channels), F32),
+            pltpu.VMEM((pairs, channels), F32),
+            pltpu.VMEM((2, pairs, channels), F32),
+            pltpu.VMEM((2, pairs, channels), F32),
+            pltpu.VMEM((2, pairs, channels), F32),
+            pltpu.VMEM((2, pairs, channels), F32),
+            pltpu.VMEM((2, pairs, channels), BF16),
+            pltpu.VMEM((2, 5, pairs, channels), F32),
+            pltpu.VMEM((2, pairs, channels), BF16),
+            pltpu.VMEM((2, pairs, channels), F32),
+            pltpu.VMEM((2, pairs, channels), F32),
+            pltpu.VMEM((pairs, channels), F32),
+            pltpu.VMEM((2, pairs, channels), BF16),
+            pltpu.VMEM((2, 5, pairs, channels), BF16),
+            pltpu.VMEM((2, 2, slices, padded, padded), BF16),
+            pltpu.VMEM((padded * 2 * slices, padded), F32),
+            pltpu.VMEM((padded * slices, padded), F32),
+            pltpu.VMEM((n, double, padded), F32),
+            pltpu.VMEM((n, single, padded), F32),
+            pltpu.VMEM((4, n, double, padded), BF16),
+            pltpu.VMEM((4, n, double, padded), BF16),
+            pltpu.VMEM((4, n, single, padded), BF16),
+            pltpu.VMEM((4, n, single, padded), BF16),
+            pltpu.VMEM((2, 6 * channels, channels), BF16),
+            pltpu.VMEM((2, n, share, channels), BF16),
+            pltpu.VMEM((2, share, channels), BF16),
+            pltpu.VMEM((2, n, share, channels), BF16),
+            pltpu.VMEM((6 * channels, channels), F32),
+            pltpu.SemaphoreType.DMA((12, n)),
+            pltpu.SemaphoreType.DMA((12, n)),
+        ],
+        compiler_params=pltpu.CompilerParams(
+            collective_id=0, has_side_effects=True, vmem_limit_bytes=40 * 2**20
+        ),
+    )(
+        pair_state,
+        chain_index.reshape(1, residues),
+        pair_mask,
+        chain_table,
+        norm_gain,
+        norm_shift,
+        projections,
+        output_weight,
+        cotangent,
+    )
+
+
+def fits(rows, residues, channels, n):
+    padded = -(-residues // LANES) * LANES
+    return (
+        channels == LANES
+        and channels % n == 0
+        and (channels // n) % 8 == 0
+        and (6 * channels // n) % 16 == 0
+        and residues % 16 == 0
+        and padded <= 2 * LANES
+        and padded - residues >= 2
+    )
+
+
+def shards(*arguments):
+    rows, residues, channels = arguments[0].shape
+    n = lax.axis_size("dap")
+    if fits(rows, residues, channels, n):
+        return fused(*arguments)
+    return sharded_ops(*arguments)
 
 
 def solution(mesh):

time: 290 us -> 103 us (0.36)
  waiting for transfers between devices: 166 us -> 0 us
  Pallas kernels: 0 us -> 93.3 us
  starting transfers between devices: 43.3 us -> 0 us
  local copies, waits for them, and re-layouts: 25.5 us -> 8.45 us
  matrix products: 15.4 us -> 0 us
  between operations: 14.9 us -> 0.67 us
  other arithmetic: 11.5 us -> 0 us
  blocking collectives: 11 us -> 0 us
    pallas_call x0 -> x1, Pallas kernels: none -> 93.3 us  [fused(): pl.pallas_call(functools.partial(fused_kernel, n, rows, residues), out_sh...]
    psum x1 -> x0, waiting for transfers between devices: 89.4 us -> none  [reduce_block(): return lax.psum((weight_grads, out_weight_grad), 'dap')]
    all_to_all x11 -> x0, waiting for transfers between devices: 77 us -> none  [the longest x2 16.7 us: block_forward(): lax.all_to_all(right_blocks, 'dap', split_axis=0, concat_axis=2, tiled=True)]
    all_to_all x11 -> x0, starting transfers between devices: 43.3 us -> none  [the longest x2 10.9 us: block_forward(): lax.all_to_all(right_blocks, 'dap', split_axis=0, concat_axis=2, tiled=True)]
    dot_general x24 -> x0, matrix products: 15.4 us -> none  [the longest x2 2.79 us: block_forward(): jnp.einsum('rnd,dc->rnc', activated, weights[4], preferred_element_type=j...]
    all_to_all x1 -> x0, blocking collectives: 11 us -> none  [block_forward(): lax.all_to_all(left_blocks, 'dap', split_axis=0, concat_axis=2, tiled=True)]
    convert_element_type x18 -> x0, local copies, waits for them, and re-layouts: 7.61 us -> none  [the longest x4 2.83 us: factor_grads(): return (left_grad.astype(jnp.bfloat16), right_grad.astype(jnp.bfloat16))]
    convert_element_type x13 -> x0, other arithmetic: 4.02 us -> none  [the longest x1 1.73 us: block_forward(): right_factor = (masked * gate_right * factor_pre[2]).astype(jnp.bfloat16)]
  transfers between devices with their start and end apart: 12 -> 0, of which waited for: 12 -> 0; matrix products, arithmetic and copies ran while one was open for 5% -> 0% of each run, Pallas kernels for 0% -> 0%
where the time goes in v1:
time: 103 us; the launch traced here: 102 us
  Pallas kernels  93.3 us (91%)
  local copies, waits for them, and re-layouts  8.45 us (8%)
    pallas_call x1, Pallas kernels, fused(): pl.pallas_call(functools.partial(fused_kernel, n, rows, residues), out_sh...  93.3 us
    unnamed x21, local copies, waits for them, and re-layouts  8.45 us

profile of v1, /device:TPU:0, one launch (start us, length us, event | category | flops | bytes accessed | tf_op | source)
XLA Modules:
  0.0 102.4 jit_solution(3250170000388667286)
XLA Ops:
  0.6 0.0 copy-start.7
  0.6 0.0 copy-start.8
  0.7 0.7 copy-done.7
  1.3 0.0 copy-done.8
  1.3 0.0 copy-start
  1.3 1.0 copy-done
  2.3 0.0 copy-start.1
  2.3 0.9 copy-done.1
  3.2 0.0 copy-start.2
  3.2 0.9 copy-done.2
  4.1 0.0 copy-start.3
  4.1 0.8 copy-done.3
  4.9 0.0 copy-start.4
  4.9 0.7 copy-done.4
  5.6 0.0 copy-start.5
  5.6 0.7 copy-done.5
  6.3 0.0 copy-start.6
  6.3 0.7 copy-done.6
  7.0 93.3 %shard_map.112 = (bf16[5,80,128]{2,1,0:T(8,128)(2,1)S(1)}, f32[2,5,128,128]{3,2,1,0:T(8,128)S(1)}, f32[2,128,128]{2,1,0:T(8,128)S(1)}) custom-call(bf16[5,80,128]{2,1,0:T(8,128)(2,1)S(1)} %copy-done.1, s32[1,80]{1,0:T(1,128)S(1)} %bitcast.1, s32[5,80]{1,0:T(8,128)S(1)} %copy-done.4, f32[2,128]{1,0:T(2,128)S(1)} %copy-done.7, f32[2,2,128]{2,1,0:T(2,128)S(1)} %copy-done.5, ...), custom_call_target="tpu_custom_call" | custom-call | tf_op jit(solution)/shard_map/pallas_call | solution.py:626
  100.3 0.6 copy.15
  100.9 0.8 copy.16
  101.7 0.7 copy.17
Async XLA Ops:
  0.6 0.7 copy-start.7
  0.6 0.7 copy-start.8
  1.3 1.0 copy-start
  2.3 0.9 copy-start.1
  3.2 0.9 copy-start.2
  4.1 0.8 copy-start.3
  4.9 0.7 copy-start.4
  5.6 0.7 copy-start.5
  6.3 0.7 copy-start.6

commit v2 on v1

--- a/solution.py
+++ b/solution.py
@@ -246,15 +246,15 @@
     n,
     rows,
     residues,
-    pair_ref,
-    chain_ref,
-    mask_ref,
-    table_ref,
-    gain_ref,
-    shift_ref,
-    proj_ref,
-    weight_ref,
-    cot_ref,
+    pair_hbm,
+    chain_hbm,
+    mask_hbm,
+    table_hbm,
+    gain_hbm,
+    shift_hbm,
+    proj_hbm,
+    weight_hbm,
+    cot_hbm,
     grad_out,
     proj_out,
     weight_out,
@@ -281,29 +281,43 @@
     wide_recv,
     thin_send,
     thin_recv,
-    sum_send,
-    sum_recv,
-    all_send,
-    all_recv,
+    early_send,
+    late_send,
+    early_recv,
+    late_recv,
+    early_share,
+    late_share,
+    early_all,
+    late_all,
     total,
     send_sem,
     recv_sem,
+    load_sem,
+    pair_ref,
+    chain_ref,
+    mask_ref,
+    table_ref,
+    gain_ref,
+    shift_ref,
+    proj_ref,
+    weight_ref,
+    cot_ref,
 ):
     channels = LANES
     slices = channels // n
     padded = factors.shape[-1]
     pairs = rows * residues
-    share = sum_recv.shape[2]
     double = 2 * slices
     me = lax.axis_index("dap")
     barrier = pltpu.get_barrier_semaphore()
 
     def each_peer(body):
         def step(index, carry):
-            body(lax.rem(me + index, n))
+            reach = n // 2 + (1 - 2 * lax.rem(index, 2)) * ((index + 1) // 2)
+            body(lax.rem(me + reach, n))
             return carry
 
-        lax.fori_loop(1, n, step, 0)
+        lax.fori_loop(0, n - 1, step, 0)
 
     def greet(peer):
         pl.semaphore_signal(
@@ -311,6 +325,24 @@
         )
 
     each_peer(greet)
+    loads = [
+        pltpu.make_async_copy(source, target, load_sem.at[place])
+        for place, (source, target) in enumerate(
+            (
+                (chain_hbm, chain_ref),
+                (mask_hbm, mask_ref),
+                (table_hbm, table_ref),
+                (pair_hbm, pair_ref),
+                (gain_hbm, gain_ref),
+                (shift_hbm, shift_ref),
+                (proj_hbm, proj_ref),
+                (weight_hbm, weight_ref),
+                (cot_hbm, cot_ref),
+            )
+        )
+    ]
+    for load in loads:
+        load.start()
 
     def copy(phase, source, target, peer, owner):
         return pltpu.make_async_remote_copy(
@@ -335,13 +367,21 @@
     def span(row):
         return pl.ds(row * residues, residues)
 
-    def to_columns(values):
-        filler = jnp.zeros((padded - residues, channels), F32)
-        full = jnp.concatenate([values, filler], axis=0) if padded > residues else values
-        return full.T.reshape(n, slices, padded)
-
-    def to_rows(blocks):
-        return blocks.reshape(channels, padded).T[:residues]
+    upper = (rows + 1) // 2
+    halves = ((0, upper), (upper, rows))
+    wide_lanes = wide_send.shape[-1]
+    thin_lanes = thin_send.shape[-1]
+
+    def to_columns(values, lanes):
+        filler = jnp.zeros((lanes - values.shape[0], channels), F32)
+        return jnp.concatenate([values, filler], axis=0).T.reshape(n, slices, lanes)
+
+    def to_rows(blocks, count):
+        return blocks.reshape(channels, blocks.shape[-1]).T[:count]
+
+    def pack(tiles, lanes):
+        filler = jnp.zeros((tiles[0].shape[0], lanes - len(tiles) * residues), F32)
+        return jnp.concatenate(tiles + [filler], axis=1)
 
     def wide(number):
         return lambda peer: wide_send.at[number, peer]
@@ -349,13 +389,8 @@
     def thin(number):
         return lambda peer: thin_send.at[number, peer]
 
-    def shares(number):
-        return lambda peer: sum_send.at[
-            number, pl.ds(pl.multiple_of(peer * share, 16), share)
-        ]
-
-    def whole_share(number):
-        return lambda peer: all_send.at[number]
+    def shares(sums, share):
+        return lambda peer: sums.at[pl.ds(pl.multiple_of(peer * share, 16), share)]
 
     exchanges = {
         0: (wide(0), wide_recv.at[0]),
@@ -366,16 +401,17 @@
         5: (wide(2), wide_recv.at[2]),
         6: (thin(3), thin_recv.at[3]),
         7: (wide(3), wide_recv.at[3]),
-        8: (shares(1), sum_recv.at[1]),
-        9: (whole_share(1), all_recv.at[1]),
-        10: (shares(0), sum_recv.at[0]),
-        11: (whole_share(0), all_recv.at[0]),
+        8: (shares(early_send, early_recv.shape[1]), early_recv),
+        9: (lambda peer: early_share, early_all),
+        10: (shares(late_send, late_recv.shape[1]), late_recv),
+        11: (lambda peer: late_share, late_all),
     }
 
     stage16[...] = jnp.zeros_like(stage16)
     stage8[...] = jnp.zeros_like(stage8)
-    rows8[...] = jnp.zeros_like(rows8)
-
+
+    for load in loads:
+        load.wait()
     chain = chain_ref[...]
     place = lax.broadcasted_iota(jnp.int32, chain.shape, 1)
     for row in range(rows):
@@ -401,12 +437,12 @@
             activated[number, span(row), :] = (normed * gain + shift).astype(BF16)
         for part in range(5):
             pre[number, part] = dot(activated[number], proj_ref[number, part], 1, 0)
-        for row in range(rows):
-            seen = mask[span(row), :]
-            left = seen * jax.nn.sigmoid(pre[number, 1, span(row)]) * pre[number, 0, span(row)]
-            right = seen * jax.nn.sigmoid(pre[number, 3, span(row)]) * pre[number, 2, span(row)]
-            both = jnp.concatenate([to_columns(left), to_columns(right)], axis=1)
-            wide_send[number, :, pl.ds(row * double, double), :] = both.astype(BF16)
+        left = mask[...] * jax.nn.sigmoid(pre[number, 1]) * pre[number, 0]
+        right = mask[...] * jax.nn.sigmoid(pre[number, 3]) * pre[number, 2]
+        both = jnp.concatenate(
+            [to_columns(left, wide_lanes), to_columns(right, wide_lanes)], axis=1
+        )
+        wide_send[number] = both.astype(BF16)
         if number == 0:
             pl.semaphore_wait(barrier, n - 1)
         send_all(2 * number, *exchanges[2 * number])
@@ -414,9 +450,11 @@
     def send_product(number):
         take_all(2 * number, *exchanges[2 * number])
         for owner in range(n):
-            stage16[pl.ds(owner * rows * double, rows * double), :] = wide_recv[
-                number, owner
-            ].astype(F32)
+            block = wide_recv[number, owner].astype(F32)
+            for row in range(rows):
+                stage16[pl.ds((owner * rows + row) * double, double), :residues] = block[
+                    :, row * residues : (row + 1) * residues
+                ]
         for channel in range(slices):
             left = stage16[pl.ds(channel, padded, stride=double), :].astype(BF16)
             right = stage16[pl.ds(slices + channel, padded, stride=double), :].astype(BF16)
@@ -425,23 +463,32 @@
             stage8[pl.ds(channel, padded, stride=slices), :] = dot(
                 left, right, 1 - number, 1 - number
             )
-        thin_rows = thin_send.shape[2]
         for owner in range(n):
-            thin_send[number, owner] = stage8[
-                pl.ds(owner * rows * slices, thin_rows), :
-            ].astype(BF16)
+            packed = [
+                pack(
+                    [
+                        stage8[pl.ds((owner * rows + row) * slices, slices), :residues]
+                        for row in range(*half)
+                    ],
+                    thin_lanes,
+                )
+                for half in halves
+            ]
+            thin_send[number, owner] = jnp.concatenate(packed, axis=0).astype(BF16)
         send_all(2 * number + 1, *exchanges[2 * number + 1])
 
     def take_product(number):
         take_all(2 * number + 1, *exchanges[2 * number + 1])
         gain, shift = gain_ref[number, 1:2, :], shift_ref[number, 1:2, :]
         rows8[...] = thin_recv[number].astype(F32)
-        for row in range(rows):
-            product = to_rows(rows8[:, pl.ds(row * slices, slices), :])
+        for place, (first, last) in enumerate(halves):
+            count = (last - first) * residues
+            product = to_rows(rows8[:, pl.ds(place * slices, slices), :], count)
             normed, inverse = norm_lanes(product)
-            normed_out[number, span(row), :] = normed
-            inverse_out[number, span(row), :] = jnp.broadcast_to(inverse, normed.shape)
-            mixture[number, span(row), :] = (normed * gain + shift).astype(BF16)
+            where = pl.ds(first * residues, count)
+            normed_out[number, where, :] = normed
+            inverse_out[number, where, :] = jnp.broadcast_to(inverse, normed.shape)
+            mixture[number, where, :] = (normed * gain + shift).astype(BF16)
 
     def take_update(number):
         update[number] = dot(mixture[number], weight_ref[number], 1, 0)
@@ -454,15 +501,17 @@
 
     def send_product_grad(number):
         gain = gain_ref[number, 1:2, :]
-        for row in range(rows):
+        packed = []
+        for first, last in halves:
+            where = pl.ds(first * residues, (last - first) * residues)
             grad = norm_lanes_back(
-                mix_grad[span(row), :],
-                normed_out[number, span(row), :],
-                inverse_out[number, span(row), :],
+                mix_grad[where, :],
+                normed_out[number, where, :],
+                inverse_out[number, where, :],
                 gain,
             )
-            rows8[:, pl.ds(row * slices, slices), :] = to_columns(grad)
-        thin_send[3 - number] = rows8[...].astype(BF16)
+            packed.append(to_columns(grad, thin_lanes))
+        thin_send[3 - number] = jnp.concatenate(packed, axis=1).astype(BF16)
         send_all(6 - 2 * number, *exchanges[6 - 2 * number])
 
     def gate_back(number):
@@ -477,20 +526,24 @@
             grad = dot(mixture[number], update_grad[number], 0, 0)
         else:
             grad = dot(activated[number], pre_grad[number, part], 0, 0)
-        sum_send[number, pl.ds(part * channels, channels), :] = (
-            grad * (1.0 / residues)
-        ).astype(BF16)
+        grad = (grad * (1.0 / residues)).astype(BF16)
+        if number == 0 and part < 4:
+            late_send[pl.ds(part * channels, channels), :] = grad
+        else:
+            slot = part if number == 1 else part + 2
+            early_send[pl.ds(slot * channels, channels), :] = grad
 
     def send_factor_grads(number):
         phase = 6 - 2 * number
         take_all(phase, *exchanges[phase])
         for owner in range(n):
             block = thin_recv[3 - number, owner].astype(F32)
-            stage8[pl.ds(owner * rows * slices, rows * slices), :] = block[: rows * slices]
-        if padded > residues:
-            stage8[pl.ds(residues * slices, (padded - residues) * slices), :] = jnp.zeros(
-                ((padded - residues) * slices, padded), F32
-            )
+            for place, (first, last) in enumerate(halves):
+                for row in range(first, last):
+                    lane = (row - first) * residues
+                    stage8[pl.ds((owner * rows + row) * slices, slices), :residues] = block[
+                        place * slices : (place + 1) * slices, lane : lane + residues
+                    ]
         for channel in range(slices):
             grad = stage8[pl.ds(channel, padded, stride=slices), :].astype(BF16)
             left, right = factors[number, 0, channel], factors[number, 1, channel]
@@ -503,25 +556,27 @@
             stage16[pl.ds(channel, padded, stride=double), :] = left_grad
             stage16[pl.ds(slices + channel, padded, stride=double), :] = right_grad
         for owner in range(n):
-            wide_send[3 - number, owner] = stage16[
-                pl.ds(owner * rows * double, rows * double), :
-            ].astype(BF16)
+            wide_send[3 - number, owner] = pack(
+                [
+                    stage16[pl.ds((owner * rows + row) * double, double), :residues]
+                    for row in range(rows)
+                ],
+                wide_lanes,
+            ).astype(BF16)
         send_all(phase + 1, *exchanges[phase + 1])
 
     def take_factor_grads(number):
         phase = 7 - 2 * number
         take_all(phase, *exchanges[phase])
         rows16[...] = wide_recv[3 - number].astype(F32)
-        for row in range(rows):
-            seen = mask[span(row), :]
-            for side in range(2):
-                grad = seen * to_rows(rows16[:, pl.ds(row * double + side * slices, slices), :])
-                gate = jax.nn.sigmoid(pre[number, 2 * side + 1, span(row)])
-                opened = grad * gate
-                pre_grad[number, 2 * side, span(row), :] = opened.astype(BF16)
-                pre_grad[number, 2 * side + 1, span(row), :] = (
-                    opened * pre[number, 2 * side, span(row)] * (1.0 - gate)
-                ).astype(BF16)
+        for side in range(2):
+            grad = to_rows(rows16[:, pl.ds(side * slices, slices), :], pairs)
+            gate = jax.nn.sigmoid(pre[number, 2 * side + 1])
+            opened = mask[...] * grad * gate
+            pre_grad[number, 2 * side] = opened.astype(BF16)
+            pre_grad[number, 2 * side + 1] = (
+                opened * pre[number, 2 * side] * (1.0 - gate)
+            ).astype(BF16)
 
     def stream_back(number):
         inner = dot(pre_grad[number, 0], proj_ref[number, 0], 1, 1)
@@ -541,23 +596,22 @@
             else:
                 grad_out[row] = grad.astype(BF16)
 
-    def send_total(number):
-        phase = 10 - 2 * number
+    def send_total(phase, parts, share):
         take_all(phase, *exchanges[phase])
-        result = sum_recv[number, 0].astype(F32)
+        result = parts[0].astype(F32)
         for owner in range(1, n):
-            result = result + sum_recv[number, owner].astype(F32)
-        all_send[number] = result.astype(BF16)
+            result = result + parts[owner].astype(F32)
+        share[...] = result.astype(BF16)
         send_all(phase + 1, *exchanges[phase + 1])
 
-    def take_total(number):
-        phase = 11 - 2 * number
+    def take_total(phase, blocks):
         take_all(phase, *exchanges[phase])
+        share = blocks.shape[1]
         for owner in range(n):
-            total[pl.ds(owner * share, share), :] = all_recv[number, owner].astype(F32)
-        for part in range(5):
-            proj_out[number, part] = total[pl.ds(part * channels, channels), :]
-        weight_out[number] = total[pl.ds(5 * channels, channels), :]
+            total[pl.ds(owner * share, share), :] = blocks[owner].astype(F32)
+
+    def part_of(slot):
+        return total[pl.ds(slot * channels, channels), :]
 
     send_factors(0)
     up[1] = cot_ref[...].reshape(pairs, channels).astype(F32)
@@ -583,22 +637,29 @@
     stream_back(1)
     mixture_back(0)
     send_product_grad(0)
+    gate_back(0)
     for part in range(4):
         weight_sum(1, part)
-    send_all(8, *exchanges[8])
-    gate_back(0)
-    send_factor_grads(0)
     weight_sum(0, 4)
     weight_sum(0, 5)
-    send_total(1)
+    send_all(8, *exchanges[8])
+    send_factor_grads(0)
+    send_total(8, early_recv, early_share)
     take_factor_grads(0)
     for part in range(4):
         weight_sum(0, part)
     send_all(10, *exchanges[10])
     stream_back(0)
-    take_total(1)
-    send_total(0)
-    take_total(0)
+    take_total(9, early_all)
+    for part in range(5):
+        proj_out[1, part] = part_of(part)
+    weight_out[1] = part_of(5)
+    proj_out[0, 4] = part_of(6)
+    weight_out[0] = part_of(7)
+    send_total(10, late_recv, late_share)
+    take_total(11, late_all)
+    for part in range(4):
+        proj_out[0, part] = part_of(part)
     for phase in range(12):
         end_all(phase, *exchanges[phase])
 
@@ -619,9 +680,10 @@
     slices = channels // n
     padded = -(-residues // LANES) * LANES
     pairs = rows * residues
-    double = rows * 2 * slices
-    single = -(-rows * slices // 16) * 16
-    share = 6 * channels // n
+    double = 2 * slices
+    wide = -(-pairs // LANES) * LANES
+    thin = -(-((rows + 1) // 2) * residues // LANES) * LANES
+    early, late = 8 * channels // n, 4 * channels // n
     vmem = pl.BlockSpec(memory_space=pltpu.VMEM)
     return pl.pallas_call(
         functools.partial(fused_kernel, n, rows, residues),
@@ -630,7 +692,7 @@
             jax.ShapeDtypeStruct((2, 5, channels, channels), F32),
             jax.ShapeDtypeStruct((2, channels, channels), F32),
         ),
-        in_specs=[vmem] * 9,
+        in_specs=[pl.BlockSpec(memory_space=pltpu.HBM)] * 9,
         out_specs=(vmem,) * 3,
         scratch_shapes=[
             pltpu.VMEM((2, pairs, channels), F32),
@@ -650,19 +712,33 @@
             pltpu.VMEM((2, 2, slices, padded, padded), BF16),
             pltpu.VMEM((padded * 2 * slices, padded), F32),
             pltpu.VMEM((padded * slices, padded), F32),
-            pltpu.VMEM((n, double, padded), F32),
-            pltpu.VMEM((n, single, padded), F32),
-            pltpu.VMEM((4, n, double, padded), BF16),
-            pltpu.VMEM((4, n, double, padded), BF16),
-            pltpu.VMEM((4, n, single, padded), BF16),
-            pltpu.VMEM((4, n, single, padded), BF16),
-            pltpu.VMEM((2, 6 * channels, channels), BF16),
-            pltpu.VMEM((2, n, share, channels), BF16),
-            pltpu.VMEM((2, share, channels), BF16),
-            pltpu.VMEM((2, n, share, channels), BF16),
-            pltpu.VMEM((6 * channels, channels), F32),
+            pltpu.VMEM((n, double, wide), F32),
+            pltpu.VMEM((n, double, thin), F32),
+            pltpu.VMEM((4, n, double, wide), BF16),
+            pltpu.VMEM((4, n, double, wide), BF16),
+            pltpu.VMEM((4, n, double, thin), BF16),
+            pltpu.VMEM((4, n, double, thin), BF16),
+            pltpu.VMEM((8 * channels, channels), BF16),
+            pltpu.VMEM((4 * channels, channels), BF16),
+            pltpu.VMEM((n, early, channels), BF16),
+            pltpu.VMEM((n, late, channels), BF16),
+            pltpu.VMEM((early, channels), BF16),
+            pltpu.VMEM((late, channels), BF16),
+            pltpu.VMEM((n, early, channels), BF16),
+            pltpu.VMEM((n, late, channels), BF16),
+            pltpu.VMEM((8 * channels, channels), F32),
             pltpu.SemaphoreType.DMA((12, n)),
             pltpu.SemaphoreType.DMA((12, n)),
+            pltpu.SemaphoreType.DMA((9,)),
+            pltpu.VMEM((rows, residues, channels), BF16),
+            pltpu.VMEM((1, residues), jnp.int32),
+            pltpu.VMEM((rows, residues), jnp.int32),
+            pltpu.VMEM((2, channels), F32),
+            pltpu.VMEM((2, 2, channels), F32),
+            pltpu.VMEM((2, 2, channels), F32),
+            pltpu.VMEM((2, 5, channels, channels), BF16),
+            pltpu.VMEM((2, channels, channels), BF16),
+            pltpu.VMEM((rows, residues, channels), BF16),
         ],
         compiler_params=pltpu.CompilerParams(
             collective_id=0, has_side_effects=True, vmem_limit_bytes=40 * 2**20
@@ -686,10 +762,10 @@
         channels == LANES
         and channels % n == 0
         and (channels // n) % 8 == 0
-        and (6 * channels // n) % 16 == 0
+        and (4 * channels // n) % 16 == 0
+        and n % 2 == 0
         and residues % 16 == 0
         and padded <= 2 * LANES
-        and padded - residues >= 2
     )
 
 

time: 103 us -> 95 us (0.922)
  Pallas kernels: 93.3 us -> 85.5 us
    pallas_call x1, Pallas kernels: 93.3 us -> 85.5 us  [fused(): pl.pallas_call(functools.partial(fused_kernel, n, rows, residues), out_sh...]
where the time goes in v2:
time: 95 us; the launch traced here: 94.7 us
  Pallas kernels  85.5 us (90%)
  local copies, waits for them, and re-layouts  8.45 us (9%)
    pallas_call x1, Pallas kernels, fused(): pl.pallas_call(functools.partial(fused_kernel, n, rows, residues), out_sh...  85.5 us
    unnamed x21, local copies, waits for them, and re-layouts  8.45 us

profile of v2, /device:TPU:0, one launch (start us, length us, event | category | flops | bytes accessed | tf_op | source)
XLA Modules:
  0.0 94.7 jit_solution(7096725601760365186)
XLA Ops:
  0.6 0.0 copy-start.7
  0.6 0.0 copy-start.8
  0.7 0.7 copy-done.7
  1.3 0.0 copy-done.8
  1.3 0.0 copy-start
  1.3 1.0 %copy-done = bf16[2,5,128,128]{3,2,1,0:T(8,128)(2,1)S(1)} copy-done((bf16[2,5,128,128]{3,2,1,0:T(8,128)(2,1)S(1)}, bf16[2,5,128,128]{3,2,1,0:T(8,128)(2,1)}, u32[]{:S(2)}) %copy-start) | copy-done | bytes 327704
  2.3 0.0 copy-start.1
  2.3 0.9 copy-done.1
  3.2 0.0 copy-start.2
  3.2 0.9 copy-done.2
  4.1 0.0 copy-start.3
  4.1 0.8 copy-done.3
  4.9 0.0 copy-start.4
  4.9 0.7 copy-done.4
  5.6 0.0 copy-start.5
  5.6 0.7 copy-done.5
  6.3 0.0 copy-start.6
  6.3 0.7 copy-done.6
  7.0 85.5 %shard_map.112 = (bf16[5,80,128]{2,1,0:T(8,128)(2,1)S(1)}, f32[2,5,128,128]{3,2,1,0:T(8,128)S(1)}, f32[2,128,128]{2,1,0:T(8,128)S(1)}) custom-call(bf16[5,80,128]{2,1,0:T(8,128)(2,1)S(1)} %copy-done.1, s32[1,80]{1,0:T(1,128)S(1)} %bitcast.1, s32[5,80]{1,0:T(8,128)S(1)} %copy-done.4, f32[2,128]{1,0:T(2,128)S(1)} %copy-done.7, f32[2,2,128]{2,1,0:T(2,128)S(1)} %copy-done.5, ...), custom_call_target="tpu_custom_call" | custom-call | tf_op jit(solution)/shard_map/pallas_call | solution.py:688
  92.5 0.6 copy.15
  93.2 0.8 copy.16
  94.0 0.7 copy.17
Async XLA Ops:
  0.6 0.7 copy-start.7
  0.6 0.7 copy-start.8
  1.3 1.0 %copy-start = (bf16[2,5,128,128]{3,2,1,0:T(8,128)(2,1)S(1)}, bf16[2,5,128,128]{3,2,1,0:T(8,128)(2,1)}, u32[]{:S(2)}) copy-start(bf16[2,5,128,128]{3,2,1,0:T(8,128)(2,1)} %proj_hbm.1) | copy-start | bytes 983044
  2.3 0.9 copy-start.1
  3.2 0.9 copy-start.2
  4.1 0.8 copy-start.3
  4.9 0.7 copy-start.4
  5.6 0.7 copy-start.5
  6.3 0.7 copy-start.6

commit v3 on v2

--- a/solution.py
+++ b/solution.py
@@ -311,13 +311,12 @@
     me = lax.axis_index("dap")
     barrier = pltpu.get_barrier_semaphore()
 
-    def each_peer(body):
+    def each_peer(body, unrolled=False):
         def step(index, carry):
-            reach = n // 2 + (1 - 2 * lax.rem(index, 2)) * ((index + 1) // 2)
-            body(lax.rem(me + reach, n))
+            body(lax.rem(me + index, n))
             return carry
 
-        lax.fori_loop(0, n - 1, step, 0)
+        lax.fori_loop(1, n, step, 0, unroll=n - 1 if unrolled else 1)
 
     def greet(peer):
         pl.semaphore_signal(
@@ -355,8 +354,8 @@
         )
 
     def send_all(phase, source_of, target):
+        each_peer(lambda peer: copy(phase, source_of(peer), target, peer, me).start(), True)
         target[me] = source_of(me)[...]
-        each_peer(lambda peer: copy(phase, source_of(peer), target, peer, me).start())
 
     def take_all(phase, source_of, target):
         each_peer(lambda peer: copy(phase, source_of(peer), target, peer, peer).wait_recv())
@@ -741,7 +740,7 @@
             pltpu.VMEM((rows, residues, channels), BF16),
         ],
         compiler_params=pltpu.CompilerParams(
-            collective_id=0, has_side_effects=True, vmem_limit_bytes=40 * 2**20
+            collective_id=0, has_side_effects=True, vmem_limit_bytes=63 * 2**20
         ),
     )(
         pair_state,

time: 95 us -> 91.1 us (0.959)
  local copies, waits for them, and re-layouts: 8.45 us -> 4.21 us
    unnamed x21 -> x5, local copies, waits for them, and re-layouts: 8.45 us -> 4.21 us
where the time goes in v3:
time: 91.1 us; the launch traced here: 90.9 us
  Pallas kernels  86 us (94%)
  local copies, waits for them, and re-layouts  4.21 us (5%)
    pallas_call x1, Pallas kernels, fused(): pl.pallas_call(functools.partial(fused_kernel, n, rows, residues), out_sh...  86 us
    unnamed x5, local copies, waits for them, and re-layouts  4.21 us

profile of v3, /device:TPU:0, one launch (start us, length us, event | category | flops | bytes accessed | tf_op | source)
XLA Modules:
  0.0 90.9 jit_solution(16160804237488053893)
XLA Ops:
  0.6 86.0 %shard_map.112 = (bf16[5,80,128]{2,1,0:T(8,128)(2,1)}, f32[2,5,128,128]{3,2,1,0:T(8,128)}, f32[2,128,128]{2,1,0:T(8,128)}) custom-call(bf16[5,80,128]{2,1,0:T(8,128)(2,1)} %pair_hbm.1, s32[1,80]{1,0:T(1,128)} %bitcast.1, s32[5,80]{1,0:T(8,128)} %mask_hbm.1, f32[2,128]{1,0:T(2,128)} %table_hbm.1, f32[2,2,128]{2,1,0:T(2,128)} %gain_hbm.1, ...), custom_call_target="tpu_custom_call" | custom-call | tf_op jit(solution)/shard_map/pallas_call | solution.py:687
  86.7 1.5 %copy.15 = bf16[5,80,128]{2,1,0:T(8,128)(2,1)} copy(bf16[5,80,128]{2,1,0:T(8,128)(2,1)} %get-tuple-element.6) | data formatting | bytes 204800
  88.2 0.0 copy-start
  88.2 2.0 %copy.16 = f32[2,5,128,128]{3,2,1,0:T(8,128)} copy(f32[2,5,128,128]{3,2,1,0:T(8,128)} %get-tuple-element.7) | data formatting | bytes 1310720
  90.2 0.0 copy-done
  90.2 0.7 copy.17
Async XLA Ops:
  88.2 2.0 %copy-start = (f32[2,128,128]{2,1,0:T(8,128)S(1)}, f32[2,128,128]{2,1,0:T(8,128)}, u32[]{:S(2)}) copy-start(f32[2,128,128]{2,1,0:T(8,128)} %get-tuple-element.8) | copy-start | bytes 393220

commit v4 on v3

--- a/solution.py
+++ b/solution.py
@@ -593,7 +593,7 @@
             if number == 1:
                 up[0, span(row), :] = grad
             else:
-                grad_out[row] = grad.astype(BF16)
+                grad_out[row] = grad
 
     def send_total(phase, parts, share):
         take_all(phase, *exchanges[phase])
@@ -607,7 +607,7 @@
         take_all(phase, *exchanges[phase])
         share = blocks.shape[1]
         for owner in range(n):
-            total[pl.ds(owner * share, share), :] = blocks[owner].astype(F32)
+            total[pl.ds(owner * share, share), :] = blocks[owner]
 
     def part_of(slot):
         return total[pl.ds(slot * channels, channels), :]
@@ -684,12 +684,12 @@
     thin = -(-((rows + 1) // 2) * residues // LANES) * LANES
     early, late = 8 * channels // n, 4 * channels // n
     vmem = pl.BlockSpec(memory_space=pltpu.VMEM)
-    return pl.pallas_call(
+    grad, proj, weight = pl.pallas_call(
         functools.partial(fused_kernel, n, rows, residues),
         out_shape=(
-            jax.ShapeDtypeStruct((rows, residues, channels), BF16),
-            jax.ShapeDtypeStruct((2, 5, channels, channels), F32),
-            jax.ShapeDtypeStruct((2, channels, channels), F32),
+            jax.ShapeDtypeStruct((rows, residues, channels), F32),
+            jax.ShapeDtypeStruct((2, 5, channels, channels), BF16),
+            jax.ShapeDtypeStruct((2, channels, channels), BF16),
         ),
         in_specs=[pl.BlockSpec(memory_space=pltpu.HBM)] * 9,
         out_specs=(vmem,) * 3,
@@ -725,7 +725,7 @@
             pltpu.VMEM((late, channels), BF16),
             pltpu.VMEM((n, early, channels), BF16),
             pltpu.VMEM((n, late, channels), BF16),
-            pltpu.VMEM((8 * channels, channels), F32),
+            pltpu.VMEM((8 * channels, channels), BF16),
             pltpu.SemaphoreType.DMA((12, n)),
             pltpu.SemaphoreType.DMA((12, n)),
             pltpu.SemaphoreType.DMA((9,)),
@@ -753,6 +753,7 @@
         output_weight,
         cotangent,
     )
+    return grad.astype(BF16), proj.astype(F32), weight.astype(F32)
 
 
 def fits(rows, residues, channels, n):

time: 91.1 us -> 90.9 us (level)
  local copies, waits for them, and re-layouts: 4.21 us -> 0.01 us
  other arithmetic: 0 us -> 4.14 us
    unnamed x5 -> x2, local copies, waits for them, and re-layouts: 4.21 us -> 0.01 us
    convert_element_type x0 -> x3, other arithmetic: none -> 4.14 us  [fused(): return (grad.astype(BF16), proj.astype(F32), weight.astype(F32))]
where the time goes in v4:
time: 90.9 us; the launch traced here: 90.7 us
  Pallas kernels  85.9 us (94%)
  other arithmetic  4.14 us (5%)
    pallas_call x1, Pallas kernels, fused(): pl.pallas_call(functools.partial(fused_kernel, n, rows, residues), out_sh...  85.9 us
    convert_element_type x3, other arithmetic, fused(): return (grad.astype(BF16), proj.astype(F32), weight.astype(F32))  4.14 us

profile of v4, /device:TPU:0, one launch (start us, length us, event | category | flops | bytes accessed | tf_op | source)
XLA Modules:
  0.0 90.7 jit_solution(16039919623086533827)
XLA Ops:
  0.6 85.9 %shard_map.112 = (f32[5,80,128]{2,1,0:T(8,128)}, bf16[2,5,128,128]{3,2,1,0:T(8,128)(2,1)}, bf16[2,128,128]{2,1,0:T(8,128)(2,1)}) custom-call(bf16[5,80,128]{2,1,0:T(8,128)(2,1)} %pair_hbm.1, s32[1,80]{1,0:T(1,128)} %bitcast.1, s32[5,80]{1,0:T(8,128)} %mask_hbm.1, f32[2,128]{1,0:T(2,128)} %table_hbm.1, f32[2,2,128]{2,1,0:T(2,128)} %gain_hbm.1, ...), custom_call_target="tpu_custom_call" | custom-call | tf_op jit(solution)/shard_map/pallas_call | solution.py:687
  86.5 1.6 %convert_element_type.9 = bf16[5,80,128]{2,1,0:T(8,128)(2,1)} convert(f32[5,80,128]{2,1,0:T(8,128)} %get-tuple-element.6) | non-fusion elementwise | flops 51200 | bytes 307200 | tf_op jit(solution)/shard_map/convert_element_type | solution.py:756
  88.1 0.0 copy-start
  88.1 1.9 %convert_element_type.10 = f32[2,5,128,128]{3,2,1,0:T(8,128)} convert(bf16[2,5,128,128]{3,2,1,0:T(8,128)(2,1)} %get-tuple-element.7) | non-fusion elementwise | flops 163840 | bytes 983040 | tf_op jit(solution)/shard_map/convert_element_type | solution.py:756
  90.0 0.0 copy-done
  90.0 0.7 convert_element_type.11
Async XLA Ops:
  88.1 1.9 %copy-start = (bf16[2,128,128]{2,1,0:T(8,128)(2,1)S(1)}, bf16[2,128,128]{2,1,0:T(8,128)(2,1)}, u32[]{:S(2)}) copy-start(bf16[2,128,128]{2,1,0:T(8,128)(2,1)} %get-tuple-element.8) | copy-start | bytes 196612
